TPU v7x, 32 devices: a whole 2x2x4 slice. The times are simulated.
32 devices in a mesh: member: 4 (over y, core), shard: 8 (over z, x).
Axes of the slice: x: 2, y: 2, z: 4, core: 2. Of those that a mesh axis runs over, the one named last changes fastest.
Arguments:
- member_grams: float32 [4, 4096, 4096], P('member', 'shard'), as said below
- member_weights: bfloat16 [4, 4096, 2304], P('member', 'shard'), may hold values from -6 to 6
Outputs:
- merged: float32 [4096, 2304], P('shard', 'member')
Inputs may be any that keep to these rules, and one draw needn't show every extreme that they name: `member_grams`: each member's matrix is symmetric positive definite.
All inputs are finite; a program needn't handle non-finite values.
Results may differ from a plain program's by a relative error of at most 0.0032.
Values may be sent and summed in bfloat16 or wider, within the bound.
A program may use at most 128 MiB of HBM per device.

v0:
```python
import jax
import jax.numpy as jnp
from jax import lax
from jax.sharding import PartitionSpec as P

ITERS = 3


shrink = 0.9


def regularize(gram_block, row_offset):
    height = gram_block.shape[-2]
    width = gram_block.shape[-1]
    row_index = lax.broadcasted_iota(jnp.int32, (height, width), 0) + row_offset
    col_index = lax.broadcasted_iota(jnp.int32, (height, width), 1)
    return jnp.where(row_index == col_index, gram_block, shrink * gram_block)


def norms_of(residual):
    return lax.psum(jnp.sum(residual * residual, axis=0), "shard")


def shards(member_grams, member_weights):
    height = member_grams.shape[1]
    regular = regularize(member_grams, lax.axis_index("shard") * height)
    gram_low = regular.astype(jnp.bfloat16)
    gram_sum = lax.psum(jnp.sum(regular, axis=0), "member")
    partial_rhs = jnp.einsum(
        "mrn,mno->ro",
        gram_low,
        lax.all_gather(member_weights, "shard", axis=1, tiled=True),
        preferred_element_type=jnp.float32,
    )
    right_side = lax.psum_scatter(partial_rhs, "member", scatter_dimension=1, tiled=True)
    merged = jnp.zeros_like(right_side)
    residual = right_side
    direction = right_side
    norm_now = norms_of(residual)
    for iteration in range(ITERS):
        images = lax.psum_scatter(
            jnp.einsum(
                "rk,rc->kc",
                gram_sum,
                direction,
                precision=lax.Precision.HIGHEST,
                preferred_element_type=jnp.float32,
            ),
            "shard",
            scatter_dimension=0,
            tiled=True,
        )
        curvature = lax.psum(jnp.sum(direction * images, axis=0), "shard")
        step_size = norm_now / curvature
        merged = merged + step_size * direction
        residual = residual - step_size * images
        if iteration + 1 < ITERS:
            norm_next = norms_of(residual)
            direction = residual + norm_next / norm_now * direction
            norm_now = norm_next
    return merged


def solution(mesh):
    return jax.shard_map(
        shards,
        mesh=mesh,
        in_specs=(P("member", "shard", None), P("member", "shard", None)),
        out_specs=P("shard", "member"),
        check_vma=False,
    )
```

profile of v0, /device:TPU:0, one launch (start us, length us, event | category | flops | bytes accessed | tf_op | source)
XLA Modules:
  0.0 1098.8 jit_solution(10664537619729423465)
XLA Ops:
  7.4 0.7 all-gather.2.cloned.1.call-update
  8.2 8.6 fusion.2
  16.8 358.1 %all-gather.2.cloned.1.call-done = bf16[1,4096,2304]{2,1,0:T(8,128)(2,1)} async-done(((bf16[1,512,2304]{2,1,0:T(8,128)(2,1)}), bf16[1,4096,2304]{2,1,0:T(8,128)(2,1)}) %all-gather.2.cloned.1.call-update) | async-done | bytes 18874384 | tf_op jit(solution)/shard_map/all_gather | solution.py:32
  374.9 18.0 %fusion = f32[512,2304]{0,1:T(8,128)} fusion(bf16[1,4096,2304]{2,1,0:T(8,128)(2,1)} %all-gather.2.cloned.1.call-done, f32[1,512,4096]{2,1,0:T(8,128)} %param.2, s32[512]{0:T(512)S(1)} %iota_add_fusion), kind=kOutput, calls=%fused_computation | convolution fusion | flops 9672065024 | bytes 31983616 | tf_op jit(solution)/shard_map/mrn,mno->ro/dot_general | solution.py:29
  393.0 47.7 %reduce-scatter.5.cloned.1.call-done = f32[512,576]{0,1:T(8,128)} async-done(((f32[512,2304]{0,1:T(8,128)}), f32[512,576]{0,1:T(8,128)}) %reduce-scatter.5.cloned.1.call-update) | async-done | bytes 1179664 | tf_op jit(solution)/shard_map/reduce_scatter | solution.py:35
  440.7 19.0 %fusion.9 = f32[4096,576]{0,1:T(8,128)} fusion(f32[512,4096]{1,0:T(8,128)} %all-reduce.3.cloned.1.call-done, f32[512,576]{0,1:T(8,128)} %reduce-scatter.5.cloned.1.call-done), kind=kOutput, calls=%fused_computation.22 | convolution fusion | flops 14495514624 | bytes 19005440 | tf_op jit(solution)/shard_map/rk,rc->kc/dot_general | solution.py:42
  459.8 163.9 %reduce-scatter.7.cloned.1.call-done = f32[512,576]{0,1:T(8,128)} async-done(((f32[4096,576]{0,1:T(8,128)}), f32[512,576]{0,1:T(8,128)}) %reduce-scatter.7.cloned.1.call-update) | async-done | bytes 1179664 | tf_op jit(solution)/shard_map/reduce_scatter | solution.py:41
  623.7 1.6 multiply_reduce_fusion.4
  625.4 19.7 %all-reduce = (f32[576]{0:T(1024)S(1)}, f32[576]{0:T(1024)S(1)}) all-reduce(f32[576]{0:T(1024)S(1)} %get-tuple-element.6, f32[576]{0:T(1024)S(1)} %get-tuple-element.5), channel_id=1, replica_groups=mesh['member'=4,'shard'=8] {'shard'}, use_global_device_ids=true, to_apply=%region_2.3 | all-reduce | flops 1152 | bytes 9216 | tf_op jit(solution)/shard_map/psum | solution.py:21
  645.1 0.3 multiply_reduce_fusion.3
  645.5 17.3 %psum.52 = f32[576]{0:T(1024)S(1)} all-reduce(f32[576]{0:T(1024)S(1)} %get-tuple-element.9), channel_id=1, replica_groups=mesh['member'=4,'shard'=8] {'shard'}, use_global_device_ids=true, to_apply=%region_8.9 | all-reduce | flops 576 | bytes 4608 | tf_op jit(solution)/shard_map/psum | solution.py:21
  663.0 18.8 %fusion.10 = f32[4096,576]{0,1:T(8,128)} fusion(f32[512,4096]{1,0:T(8,128)} %all-reduce.3.cloned.1.call-done, f32[512,576]{0,1:T(8,128)S(1)} %multiply_add_fusion.2), kind=kOutput, calls=%fused_computation.23 | convolution fusion | flops 14495514624 | bytes 19005440 | tf_op jit(solution)/shard_map/rk,rc->kc/dot_general | solution.py:42
  681.8 162.6 %reduce-scatter.9.cloned.1.call-done = f32[512,576]{0,1:T(8,128)} async-done(((f32[4096,576]{0,1:T(8,128)}), f32[512,576]{0,1:T(8,128)}) %reduce-scatter.9.cloned.1.call-update) | async-done | bytes 1179664 | tf_op jit(solution)/shard_map/reduce_scatter | solution.py:41
  844.5 1.5 multiply_reduce_fusion.2
  845.9 19.4 %psum.53 = f32[576]{0:T(1024)S(1)} all-reduce(f32[576]{0:T(1024)S(1)} %multiply_reduce_fusion.2), channel_id=1, replica_groups=mesh['member'=4,'shard'=8] {'shard'}, use_global_device_ids=true, to_apply=%region_11.12 | all-reduce | flops 576 | bytes 4608 | tf_op jit(solution)/shard_map/psum | solution.py:53
  865.4 2.2 multiply_reduce_fusion.1
  867.6 17.2 %psum.54 = f32[576]{0:T(1024)S(1)} all-reduce(f32[576]{0:T(1024)} %multiply_reduce_fusion.1), channel_id=1, replica_groups=mesh['member'=4,'shard'=8] {'shard'}, use_global_device_ids=true, to_apply=%region_13.14 | all-reduce | flops 576 | bytes 4608 | tf_op jit(solution)/shard_map/psum | solution.py:21
  884.8 1.9 multiply_add_fusion.1
  886.7 18.8 %fusion.11 = f32[4096,576]{0,1:T(8,128)} fusion(f32[512,4096]{1,0:T(8,128)} %all-reduce.3.cloned.1.call-done, f32[512,576]{0,1:T(8,128)S(1)} %multiply_add_fusion.1), kind=kOutput, calls=%fused_computation.24 | convolution fusion | flops 14495514624 | bytes 19005440 | tf_op jit(solution)/shard_map/rk,rc->kc/dot_general | solution.py:42
  905.5 162.6 %reduce-scatter.11.cloned.1.call-done = f32[512,576]{0,1:T(8,128)} async-done(((f32[4096,576]{0,1:T(8,128)}), f32[512,576]{0,1:T(8,128)}) %reduce-scatter.11.cloned.1.call-update) | async-done | bytes 1179664 | tf_op jit(solution)/shard_map/reduce_scatter | solution.py:41
  1068.1 1.5 multiply_reduce_fusion
  1069.6 20.0 %psum.55 = f32[576]{0:T(1024)} all-reduce(f32[576]{0:T(1024)S(1)} %multiply_reduce_fusion), channel_id=1, replica_groups=mesh['member'=4,'shard'=8] {'shard'}, use_global_device_ids=true, to_apply=%region_16.17 | all-reduce | flops 576 | bytes 4608 | tf_op jit(solution)/shard_map/psum | solution.py:53
  1089.6 0.7 div.19
  1090.3 1.3 multiply_add_fusion
  (24 shorter events, 0.5 us)
Async XLA Ops:
  7.4 367.6 %all-gather.2.cloned.1.call-start = ((), (), s32[]{:S(2)}) async-start(), calls=%async_computation.4 | async-start | bytes 21233664 | tf_op jit(solution)/shard_map/all_gather | solution.py:32
  8.1 384.9 %all-reduce.3.cloned.1.call-start = ((), (), s32[]{:S(2)}) async-start(), calls=%async_computation.6 | async-start | bytes 16777216 | tf_op jit(solution)/shard_map/psum | solution.py:28
  16.7 424.0 %reduce-scatter.5.cloned.1.call-start = ((), (), s32[]{:S(2)}) async-start(), calls=%async_computation.5 | async-start | bytes 5898240 | tf_op jit(solution)/shard_map/reduce_scatter | solution.py:35
  392.9 230.8 %reduce-scatter.7.cloned.1.call-start = ((), (), s32[]{:S(2)}) async-start(), calls=%async_computation.7 | async-start | bytes 10616832 | tf_op jit(solution)/shard_map/reduce_scatter | solution.py:41
  459.7 164.0 %copy-start = (f32[512,576]{0,1:T(8,128)S(1)}, f32[512,576]{0,1:T(8,128)}, u32[]{:S(2)}) copy-start(f32[512,576]{0,1:T(8,128)} %reduce-scatter.5.cloned.1.call-done) | copy-start | bytes 3538948
  459.8 384.7 %reduce-scatter.9.cloned.1.call-start = ((), (), s32[]{:S(2)}) async-start(), calls=%async_computation.8 | async-start | bytes 10616832 | tf_op jit(solution)/shard_map/reduce_scatter | solution.py:41
  623.7 21.4 %copy-start.2 = (f32[512,576]{0,1:T(8,128)S(1)}, f32[512,576]{0,1:T(8,128)}, u32[]{:S(2)}) copy-start(f32[512,576]{0,1:T(8,128)} %reduce-scatter.7.cloned.1.call-done) | copy-start | bytes 3538948
  645.5 219.9 %copy-start.1 = (f32[512,576]{0,1:T(8,128)}, f32[512,576]{0,1:T(8,128)S(1)}, u32[]{:S(2)}) copy-start(f32[512,576]{0,1:T(8,128)S(1)} %get-tuple-element.10) | copy-start | bytes 3538948
  681.8 386.4 %reduce-scatter.11.cloned.1.call-start = ((), (), s32[]{:S(2)}) async-start(), calls=%async_computation.9 | async-start | bytes 10616832 | tf_op jit(solution)/shard_map/reduce_scatter | solution.py:41
Sparse Core Ops, SparseCore 0:
  9.7 365.1 all-gather.1
  459.9 163.8 reduce-scatter.6
  681.9 162.5 reduce-scatter.8
  905.6 162.4 reduce-scatter.10
Sparse Core Ops, SparseCore 1:
  16.8 155.3 all-reduce.2
  393.0 47.6 reduce-scatter.4
where the time goes:
time: 1100 us
  waiting for transfers between devices  896 us (81%)
  blocking collectives  93.7 us (9%)
  matrix products  74.6 us (7%)
  other arithmetic  19.8 us (2%)
  between operations  14.7 us (1%)
    reduce_scatter x3, waiting for transfers between devices, shards(): lax.psum_scatter(jnp.einsum('rk,rc->kc', gram_sum, direction, precision=l...  489 us
    all_gather x1, waiting for transfers between devices, shards(): lax.all_gather(member_weights, 'shard', axis=1, tiled=True)  358 us
    dot_general x3, matrix products, shards(): jnp.einsum('rk,rc->kc', gram_sum, direction, precision=lax.Precision.HIGH...  56.6 us
    psum x3, blocking collectives, norms_of(): return lax.psum(jnp.sum(residual * residual, axis=0), 'shard')  54.2 us
    reduce_scatter x1, waiting for transfers between devices, shards(): lax.psum_scatter(partial_rhs, 'member', scatter_dimension=1, tiled=True)  47.7 us
    psum x2, blocking collectives, shards(): curvature = lax.psum(jnp.sum(direction * images, axis=0), 'shard')  39.5 us
  transfers between devices with their start and end apart: 6, of which 5 were waited for; matrix products, arithmetic and copies ran while one was open for 2% of the time, Pallas kernels for 0%

commit v1 on v0

--- a/solution.py
+++ b/solution.py
@@ -33,22 +33,16 @@
         preferred_element_type=jnp.float32,
     )
     right_side = lax.psum_scatter(partial_rhs, "member", scatter_dimension=1, tiled=True)
+    gram_used = gram_sum.astype(jnp.bfloat16)
     merged = jnp.zeros_like(right_side)
     residual = right_side
     direction = right_side
     norm_now = norms_of(residual)
     for iteration in range(ITERS):
-        images = lax.psum_scatter(
-            jnp.einsum(
-                "rk,rc->kc",
-                gram_sum,
-                direction,
-                precision=lax.Precision.HIGHEST,
-                preferred_element_type=jnp.float32,
-            ),
-            "shard",
-            scatter_dimension=0,
-            tiled=True,
+        images = jnp.dot(
+            gram_used,
+            lax.all_gather(direction.astype(jnp.bfloat16), "shard", axis=0, tiled=True),
+            preferred_element_type=jnp.float32,
         )
         curvature = lax.psum(jnp.sum(direction * images, axis=0), "shard")
         step_size = norm_now / curvature

time: 1100 us -> 878 us (0.80)
  waiting for transfers between devices: 896 us -> 565 us
  blocking collectives: 93.7 us -> 241 us
  matrix products: 74.6 us -> 39.1 us
    reduce_scatter x3 -> x0, waiting for transfers between devices: 489 us -> none  [shards(): lax.psum_scatter(jnp.einsum('rk,rc->kc', gram_sum, direction, precision=l...]
    all_gather x0 -> x3, waiting for transfers between devices: none -> 159 us  [shards(): lax.all_gather(direction.astype(jnp.bfloat16), 'shard', axis=0, tiled=True)]
    psum x0 -> x1, blocking collectives: none -> 147 us  [shards(): gram_sum = lax.psum(jnp.sum(regular, axis=0), 'member')]
    dot_general x3, matrix products: 56.6 us -> 21 us  [shards(): jnp.dot(gram_used, lax.all_gather(direction.astype(jnp.bfloat16), 'shard'...]
  transfers between devices with their start and end apart: 6 -> 5, of which waited for: 5 -> 4; matrix products, arithmetic and copies ran while one was open for 2% -> 1% of each run, Pallas kernels for 0% -> 0%
where the time goes in v1:
time: 878 us
  waiting for transfers between devices  565 us (64%)
  blocking collectives  241 us (27%)
  matrix products  39.1 us (4%)
  other arithmetic  19.2 us (2%)
  between operations  13.2 us (2%)
    all_gather x1, waiting for transfers between devices, shards(): lax.all_gather(member_weights, 'shard', axis=1, tiled=True)  367 us
    all_gather x3, waiting for transfers between devices, shards(): lax.all_gather(direction.astype(jnp.bfloat16), 'shard', axis=0, tiled=True)  159 us
    psum x1, blocking collectives, shards(): gram_sum = lax.psum(jnp.sum(regular, axis=0), 'member')  147 us
    psum x3, blocking collectives, norms_of(): return lax.psum(jnp.sum(residual * residual, axis=0), 'shard')  56.6 us
    reduce_scatter x1, waiting for transfers between devices, shards(): lax.psum_scatter(partial_rhs, 'member', scatter_dimension=1, tiled=True)  38.6 us
    psum x2, blocking collectives, shards(): curvature = lax.psum(jnp.sum(direction * images, axis=0), 'shard')  37.3 us
    dot_general x3, matrix products, shards(): jnp.dot(gram_used, lax.all_gather(direction.astype(jnp.bfloat16), 'shard'...  21 us
    dot_general x1, matrix products, shards(): jnp.einsum('mrn,mno->ro', gram_low, lax.all_gather(member_weights, 'shard...  18.1 us
  transfers between devices with their start and end apart: 5, of which 4 were waited for; matrix products, arithmetic and copies ran while one was open for 1% of the time, Pallas kernels for 0%

profile of v1, /device:TPU:0, one launch (start us, length us, event | category | flops | bytes accessed | tf_op | source)
XLA Modules:
  0.0 877.7 jit_solution(16427503228007680102)
XLA Ops:
  6.5 0.7 all-gather.5.cloned.1.call-update
  7.3 366.8 %all-gather.5.cloned.1.call-done = bf16[1,4096,2304]{2,1,0:T(8,128)(2,1)} async-done(((bf16[1,512,2304]{2,1,0:T(8,128)(2,1)}), bf16[1,4096,2304]{2,1,0:T(8,128)(2,1)}) %all-gather.5.cloned.1.call-update) | async-done | bytes 18874384 | tf_op jit(solution)/shard_map/all_gather | solution.py:32
  374.1 18.1 %fusion = f32[512,2304]{0,1:T(8,128)} fusion(bf16[1,4096,2304]{2,1,0:T(8,128)(2,1)} %all-gather.5.cloned.1.call-done, f32[1,512,4096]{2,1,0:T(8,128)} %param.2, s32[512]{0:T(512)S(1)} %iota_add_fusion), kind=kOutput, calls=%fused_computation | convolution fusion | flops 9672065024 | bytes 31983616 | tf_op jit(solution)/shard_map/mrn,mno->ro/dot_general | solution.py:29
  392.2 0.0 all-gather.7.cloned.1.call-start
  392.2 9.3 %fusion.2 = f32[512,4096]{1,0:T(8,128)} fusion(f32[1,512,4096]{2,1,0:T(8,128)} %param.2, s32[512]{0:T(512)S(1)} %iota_add_fusion), kind=kLoop, calls=%fused_computation.4 | loop fusion | flops 6291456 | bytes 16779264 | tf_op jit(solution)/shard_map/reduce_sum | solution.py:28
  401.6 38.6 %reduce-scatter.2.cloned.1.call-done = f32[512,576]{0,1:T(8,128)} async-done(((f32[512,2304]{0,1:T(8,128)}), f32[512,576]{0,1:T(8,128)}) %reduce-scatter.2.cloned.1.call-update) | async-done | bytes 1179664 | tf_op jit(solution)/shard_map/reduce_scatter | solution.py:35
  440.1 2.2 convert_element_type.17
  442.4 147.1 %all-reduce.2 = bf16[512,4096]{1,0:T(8,128)(2,1)} all-reduce(f32[512,4096]{1,0:T(8,128)} %fusion.2), channel_id=1, replica_groups=mesh['member'=4,'shard'=8] {'member'}, use_global_device_ids=true, to_apply=%region_3.4 | all-reduce | flops 2097152 | bytes 12582912 | tf_op jit(solution)/shard_map/psum | solution.py:28
  589.4 6.5 multiply_reduce_fusion.3
  595.9 21.7 %all-reduce = (f32[576]{0:T(1024)S(1)}, f32[576]{0:T(1024)S(1)}) all-reduce(f32[576]{0:T(1024)S(1)} %get-tuple-element.6, f32[576]{0:T(1024)S(1)} %get-tuple-element.5), channel_id=1, replica_groups=mesh['member'=4,'shard'=8] {'shard'}, use_global_device_ids=true, to_apply=%region_2.3 | all-reduce | flops 1152 | bytes 9216 | tf_op jit(solution)/shard_map/psum | solution.py:21
  617.6 0.3 multiply_reduce_fusion.2
  618.0 17.1 %psum.52 = f32[576]{0:T(1024)S(1)} all-reduce(f32[576]{0:T(1024)S(1)} %get-tuple-element.13), channel_id=1, replica_groups=mesh['member'=4,'shard'=8] {'shard'}, use_global_device_ids=true, to_apply=%region_7.8 | all-reduce | flops 576 | bytes 4608 | tf_op jit(solution)/shard_map/psum | solution.py:21
  635.1 1.0 fusion.16
  636.2 0.2 all-gather.11.cloned.1.call-start
  636.4 79.6 %all-gather.9.cloned.1.call-done = bf16[4096,576]{0,1:T(8,128)(2,1)} async-done(((bf16[512,576]{0,1:T(8,128)(2,1)}), bf16[4096,576]{0,1:T(8,128)(2,1)}) %all-gather.9.cloned.1.call-update) | async-done | bytes 4718608 | tf_op jit(solution)/shard_map/all_gather | solution.py:44
  715.9 7.3 multiply_reduce_fusion.1
  723.2 18.6 %psum.53 = f32[576]{0:T(1024)S(1)} all-reduce(f32[576]{0:T(1024)S(1)} %get-tuple-element.16), channel_id=1, replica_groups=mesh['member'=4,'shard'=8] {'shard'}, use_global_device_ids=true, to_apply=%region_9.10 | all-reduce | flops 576 | bytes 4608 | tf_op jit(solution)/shard_map/psum | solution.py:47
  741.8 2.2 multiply_reduce_fusion
  744.0 17.8 %psum.54 = f32[576]{0:T(1024)S(1)} all-reduce(f32[576]{0:T(1024)} %multiply_reduce_fusion), channel_id=1, replica_groups=mesh['member'=4,'shard'=8] {'shard'}, use_global_device_ids=true, to_apply=%region_11.12 | all-reduce | flops 576 | bytes 4608 | tf_op jit(solution)/shard_map/psum | solution.py:21
  761.8 2.8 fusion.15
  764.6 79.3 %all-gather.11.cloned.1.call-done = bf16[4096,576]{0,1:T(8,128)(2,1)} async-done(((bf16[512,576]{0,1:T(8,128)(2,1)}), bf16[4096,576]{0,1:T(8,128)(2,1)}) %all-gather.11.cloned.1.call-update) | async-done | bytes 4718608 | tf_op jit(solution)/shard_map/all_gather | solution.py:44
  843.9 7.3 fusion.8
  851.2 18.7 %psum.55 = f32[576]{0:T(1024)S(1)} all-reduce(f32[576]{0:T(1024)} %fusion.8), channel_id=1, replica_groups=mesh['member'=4,'shard'=8] {'shard'}, use_global_device_ids=true, to_apply=%region_13.14 | all-reduce | flops 576 | bytes 4608 | tf_op jit(solution)/shard_map/psum | solution.py:47
  869.9 1.3 multiply_add_fusion
  (18 shorter events, 0.2 us)
Async XLA Ops:
  6.5 367.5 %all-gather.5.cloned.1.call-start = ((), (), s32[]{:S(2)}) async-start(), calls=%async_computation.1 | async-start | bytes 21233664 | tf_op jit(solution)/shard_map/all_gather | solution.py:32
  7.3 432.9 %reduce-scatter.2.cloned.1.call-start = ((), (), s32[]{:S(2)}) async-start(), calls=%async_computation.2 | async-start | bytes 5898240 | tf_op jit(solution)/shard_map/reduce_scatter | solution.py:35
  392.2 197.3 %all-gather.7.cloned.1.call-start = ((), (), s32[]{:S(2)}) async-start(), calls=%async_computation.3 | async-start | bytes 5308416 | tf_op jit(solution)/shard_map/all_gather | solution.py:44
  442.3 147.1 %copy-start = (f32[512,576]{0,1:T(8,128)S(1)}, f32[512,576]{0,1:T(8,128)}, u32[]{:S(2)}) copy-start(f32[512,576]{0,1:T(8,128)} %reduce-scatter.2.cloned.1.call-done) | copy-start | bytes 3538948
  442.3 273.6 %all-gather.9.cloned.1.call-start = ((), (), s32[]{:S(2)}) async-start(), calls=%async_computation.4 | async-start | bytes 5308416 | tf_op jit(solution)/shard_map/all_gather | solution.py:44
  636.2 207.7 %all-gather.11.cloned.1.call-start = ((), (), s32[]{:S(2)}) async-start(), calls=%async_computation.5 | async-start | bytes 5308416 | tf_op jit(solution)/shard_map/all_gather | solution.py:44
  843.9 26.0 %copy-start.1 = (f32[512,576]{0,1:T(8,128)S(1)}, f32[512,576]{0,1:T(8,128)}, u32[]{:S(2)}) copy-start(f32[512,576]{0,1:T(8,128)} %get-tuple-element.10) | copy-start | bytes 3538948
Sparse Core Ops, SparseCore 0:
  8.9 365.1 all-gather.4
  392.3 47.8 reduce-scatter.1
  442.4 80.9 all-gather.6
  636.3 79.6 all-gather.8
  764.7 79.1 all-gather.10

commit v2 on v1

v2 whole, which is shorter than its diff:
```python
import functools

import jax
import jax.numpy as jnp
from jax import lax
from jax.experimental import pallas as pl
from jax.experimental.pallas import tpu as pltpu
from jax.sharding import PartitionSpec as P

ITERS = 3
MESH = pl.DeviceIdType.MESH


shrink = 0.9


def regularize(gram_block, row_offset):
    height = gram_block.shape[-2]
    width = gram_block.shape[-1]
    row_index = lax.broadcasted_iota(jnp.int32, (height, width), 0) + row_offset
    col_index = lax.broadcasted_iota(jnp.int32, (height, width), 1)
    return jnp.where(row_index == col_index, gram_block, shrink * gram_block)


def greet_all(count):
    me = lax.axis_index("shard")
    barrier = pltpu.get_barrier_semaphore()

    def greet(step, carry):
        pl.semaphore_signal(
            barrier, inc=1, device_id={"shard": lax.rem(me + step, count)}, device_id_type=MESH
        )
        return carry

    lax.fori_loop(1, count, greet, 0)
    pl.semaphore_wait(barrier, count - 1)


def gather_multiply(lines, across, chunks, tile, gram, full, total, recv_sem, line_sem, cross_sem):
    me = lax.axis_index("shard")
    z, x = me // across, lax.rem(me, across)
    height = full.shape[1]
    rows = height // chunks

    def piece(block, k):
        return full.at[block, pl.ds(k * rows, rows)]

    def inside(place):
        return (place >= 0) & (place < lines)

    def line_copy(block, way, t, k, target):
        return pltpu.make_async_remote_copy(
            src_ref=piece(block, k), dst_ref=piece(block, k),
            send_sem=line_sem.at[way, t, k], recv_sem=recv_sem.at[block, k],
            device_id={"shard": target}, device_id_type=MESH,
        )

    def cross_copy(block, way, t, hop, k, target):
        return pltpu.make_async_remote_copy(
            src_ref=piece(block, k), dst_ref=piece(block, k),
            send_sem=cross_sem.at[way, t, hop - 1, k], recv_sem=recv_sem.at[block, k],
            device_id={"shard": target}, device_id_type=MESH,
        )

    def sends(t, act, receive):
        for k in range(chunks):
            for way, sign in enumerate((1, -1)):
                source = z - sign * t
                block = source * across + x
                here = inside(source)
                following = z + sign
                if receive:
                    @pl.when(here & (t > 0))
                    def _():
                        line_copy(block, way, t, k, me).wait_recv()

                @pl.when(here & inside(following))
                def _():
                    act(line_copy(block, way, t, k, following * across + x))

                @pl.when(here & ((t > 0) | (sign > 0)))
                def _():
                    for hop in range(1, across):
                        act(cross_copy(block, way, t, hop, k, z * across + lax.rem(x + hop, across)))

    def multiply(t):
        for way, sign in enumerate((1, -1)):
            source = z - sign * t

            @pl.when(inside(source) & ((t > 0) | (sign > 0)))
            def _():
                def one(hop, carry):
                    block = source * across + lax.rem(x + hop, across)

                    @pl.when(hop > 0)
                    def _():
                        for k in range(chunks):
                            line_copy(block, way, t, k, me).wait_recv()

                    left = gram[:, pl.ds(pl.multiple_of(block * height, height), height)]
                    if tile == total.shape[1]:
                        total[...] += jnp.dot(left, full[block], preferred_element_type=jnp.float32)
                    else:
                        def columns(j, inner):
                            at = pl.ds(pl.multiple_of(j * tile, tile), tile)
                            total[:, at] += jnp.dot(
                                left, full[block, :, at], preferred_element_type=jnp.float32
                            )
                            return inner

                        lax.fori_loop(0, total.shape[1] // tile, columns, 0)
                    return carry

                lax.fori_loop(0, across, one, 0)

    def step(t, carry):
        sends(t, lambda copy: copy.start(), True)

        @pl.when(t > 0)
        def _():
            multiply(t - 1)

        return carry

    lax.fori_loop(0, lines, step, 0)
    multiply(jnp.int32(lines - 1))

    def finish(t, carry):
        sends(t, lambda copy: copy.wait_send(), False)
        return carry

    lax.fori_loop(0, lines, finish, 0)


def weigh_kernel(lines, across, chunks, tile, gram, weights, total, full, recv_sem, line_sem, cross_sem):
    me = lax.axis_index("shard")
    full[me] = weights[...]
    total[...] = jnp.zeros_like(total)
    greet_all(lines * across)
    gather_multiply(lines, across, chunks, tile, gram, full, total, recv_sem, line_sem, cross_sem)


def solve_kernel(lines, across, chunks, gram, right_side, merged, full, residual, direction, image,
                 product, sums, recv_sem, line_sem, cross_sem, sums_send, sums_recv):
    me = lax.axis_index("shard")
    count = lines * across
    width = residual.shape[1]

    def sum_copy(which, slot, step, target):
        return pltpu.make_async_remote_copy(
            src_ref=sums.at[which, slot], dst_ref=sums.at[which, slot],
            send_sem=sums_send.at[which, step], recv_sem=sums_recv.at[which, slot],
            device_id={"shard": target}, device_id_type=MESH,
        )

    def sum_start(which, values):
        sums[which, me] = jnp.sum(values.reshape(-1, 8, width), axis=0)

        def send(step, carry):
            sum_copy(which, me, step, lax.rem(me + step, count)).start()
            return carry

        lax.fori_loop(1, count, send, 0)

    def sum_finish(which):
        def receive(step, carry):
            sum_copy(which, lax.rem(me + step, count), step, me).wait_recv()
            return carry

        lax.fori_loop(1, count, receive, 0)
        result = jnp.sum(jnp.sum(sums[which], axis=0), axis=0, keepdims=True)

        def sent(step, carry):
            sum_copy(which, me, step, lax.rem(me + step, count)).wait_send()
            return carry

        lax.fori_loop(1, count, sent, 0)
        return result

    greet_all(count)
    residual[...] = right_side[...]
    merged[...] = jnp.zeros_like(merged)
    norm_now = None
    for iteration in range(ITERS):
        now = residual[...]
        full[me] = now.astype(jnp.bfloat16)
        sum_start(2 * iteration, now * now)
        product[...] = jnp.zeros_like(product)
        gather_multiply(lines, across, chunks, width, gram, full, product, recv_sem, line_sem, cross_sem)
        norm_next = sum_finish(2 * iteration)
        if iteration == 0:
            direction[...] = residual[...]
            image[...] = product[...]
        else:
            ratio = norm_next / norm_now
            direction[...] = residual[...] + ratio * direction[...]
            image[...] = product[...] + ratio * image[...]
        norm_now = norm_next
        sum_start(2 * iteration + 1, direction[...] * image[...])
        step_size = norm_now / sum_finish(2 * iteration + 1)
        merged[...] += step_size * direction[...]
        if iteration + 1 < ITERS:
            residual[...] -= step_size * image[...]


def gather_scratch(lines, across, chunks):
    return [
        pltpu.SemaphoreType.DMA((lines * across, chunks)),
        pltpu.SemaphoreType.DMA((2, lines, chunks)),
        pltpu.SemaphoreType.DMA((2, lines, max(across - 1, 1), chunks)),
    ]


def widest(width):
    for tile in range(width // 128 * 128, 0, -128):
        if tile <= 768 and width % tile == 0:
            return tile
    return width


def shards(lines, across, member_grams, member_weights):
    height = member_grams.shape[1]
    features = member_weights.shape[2]
    count = lines * across
    regular = regularize(member_grams[0], lax.axis_index("shard") * height)
    gram_low = regular.astype(jnp.bfloat16)
    gram_sum = lax.psum(regular, "member").astype(jnp.bfloat16)
    vmem = pl.BlockSpec(memory_space=pltpu.VMEM)
    partial_rhs = pl.pallas_call(
        functools.partial(weigh_kernel, lines, across, 4, widest(features)),
        out_shape=jax.ShapeDtypeStruct((height, features), jnp.float32),
        in_specs=[vmem, vmem],
        out_specs=vmem,
        scratch_shapes=[pltpu.VMEM((count, height, features), jnp.bfloat16)]
        + gather_scratch(lines, across, 4),
        compiler_params=pltpu.CompilerParams(
            collective_id=0, has_side_effects=True, vmem_limit_bytes=48 << 20
        ),
    )(gram_low, member_weights[0])
    right_side = lax.psum_scatter(partial_rhs, "member", scatter_dimension=1, tiled=True)
    width = right_side.shape[1]
    state = pltpu.VMEM((height, width), jnp.float32)
    return pl.pallas_call(
        functools.partial(solve_kernel, lines, across, 2),
        out_shape=jax.ShapeDtypeStruct((height, width), jnp.float32),
        in_specs=[vmem, vmem],
        out_specs=vmem,
        scratch_shapes=[pltpu.VMEM((count, height, width), jnp.bfloat16)]
        + [state] * 4
        + [pltpu.VMEM((2 * ITERS, count, 8, width), jnp.float32)]
        + gather_scratch(lines, across, 2)
        + [pltpu.SemaphoreType.DMA((2 * ITERS, count)), pltpu.SemaphoreType.DMA((2 * ITERS, count))],
        compiler_params=pltpu.CompilerParams(
            collective_id=1, has_side_effects=True, vmem_limit_bytes=40 << 20
        ),
    )(gram_sum, right_side)


def solution(mesh):
    count = mesh.shape["shard"]
    places = {getattr(device, "coords", (0,))[0] for device in mesh.devices.flat}
    across = len(places) if count % len(places) == 0 else 1
    return jax.shard_map(
        functools.partial(shards, count // across, across),
        mesh=mesh,
        in_specs=(P("member", "shard", None), P("member", "shard", None)),
        out_specs=P("shard", "member"),
        check_vma=False,
    )
```

time: 878 us -> 623 us (0.71)
  waiting for transfers between devices: 565 us -> 0.02 us
  Pallas kernels: 0 us -> 418 us
  blocking collectives: 241 us -> 172 us
  matrix products: 39.1 us -> 0 us
  local copies, waits for them, and re-layouts: 0.01 us -> 11.4 us
  other arithmetic: 19.2 us -> 7.9 us
    all_gather x4 -> x0, waiting for transfers between devices: 526 us -> none  [the longest x1 367 us: shards(): lax.all_gather(member_weights, 'shard', axis=1, tiled=True)]
    pallas_call x0 -> x2, Pallas kernels: none -> 418 us  [the longest x1 217 us: shards(): pl.pallas_call(functools.partial(weigh_kernel, lines, across, 4, widest(f...]
    psum x6 -> x1, blocking collectives: 241 us -> 172 us  [shards(): gram_sum = lax.psum(regular, 'member').astype(jnp.bfloat16)]
    dot_general x4 -> x0, matrix products: 39.1 us -> none  [the longest x3 21 us: shards(): jnp.dot(gram_used, lax.all_gather(direction.astype(jnp.bfloat16), 'shard'...]
    reduce_scatter x1 -> x0, waiting for transfers between devices: 38.6 us -> none  [shards(): lax.psum_scatter(partial_rhs, 'member', scatter_dimension=1, tiled=True)]
    reduce_sum x3 -> x0, other arithmetic: 11.9 us -> none  [the longest x1 9.34 us: shards(): gram_sum = lax.psum(jnp.sum(regular, axis=0), 'member')]
    unnamed x4 -> x6, local copies, waits for them, and re-layouts: 0.01 us -> 9.95 us
  transfers between devices with their start and end apart: 5 -> 1, of which waited for: 4 -> 0; matrix products, arithmetic and copies ran while one was open for 1% -> 0% of each run, Pallas kernels for 0% -> 0%
where the time goes in v2:
time: 623 us; the launch traced here: 622 us
  Pallas kernels  418 us (67%)
  blocking collectives  172 us (28%)
  between operations  13.4 us (2%)
  local copies, waits for them, and re-layouts  11.4 us (2%)
  other arithmetic  7.9 us (1%)
    pallas_call x1, Pallas kernels, shards(): pl.pallas_call(functools.partial(weigh_kernel, lines, across, 4, widest(f...  217 us
    pallas_call x1, Pallas kernels, shards(): pl.pallas_call(functools.partial(solve_kernel, lines, across, 2), out_sha...  201 us
    psum x1, blocking collectives, shards(): gram_sum = lax.psum(regular, 'member').astype(jnp.bfloat16)  172 us
  transfers between devices with their start and end apart: 1, of which 0 were waited for; matrix products, arithmetic and copies ran while one was open for 0% of the time, Pallas kernels for 0%

profile of v2, /device:TPU:0, one launch (start us, length us, event | category | flops | bytes accessed | tf_op | source)
XLA Modules:
  0.0 622.5 jit_solution(18124918013927893785)
XLA Ops:
  6.5 0.0 reduce-scatter.4.cloned.1.call-start
  6.5 0.0 copy-start.1
  6.5 7.9 %fusion = (bf16[512,4096]{1,0:T(8,128)(2,1)}, f32[512,4096]{1,0:T(8,128)}) fusion(f32[1,512,4096]{2,1,0:T(8,128)} %param.2, s32[512]{0:T(512)S(1)} %iota_add_fusion), kind=kLoop, calls=%fused_computation.3 | loop fusion | flops 8388608 | bytes 20973568 | tf_op jit(solution)/shard_map/convert_element_type | solution.py:226
  14.4 0.0 copy-done.1
  14.4 216.7 %shard_map.28 = f32[512,2304]{1,0:T(8,128)} custom-call(bf16[512,4096]{1,0:T(8,128)(2,1)} %get-tuple-element.5.gram, bf16[512,2304]{1,0:T(8,128)(2,1)S(1)} %bitcast.6), custom_call_target="tpu_custom_call" | custom-call | tf_op jit(solution)/shard_map/pallas_call | solution.py:229
  231.2 6.1 copy.5
  237.3 0.0 reduce-scatter.4.cloned.1.call-update
  237.3 172.0 %all-reduce.1.gram = bf16[512,4096]{1,0:T(8,128)(2,1)} all-reduce(f32[512,4096]{1,0:T(8,128)} %get-tuple-element.6), channel_id=1, replica_groups=mesh['member'=4,'shard'=8] {'member'}, use_global_device_ids=true, to_apply=%region_0.1 | all-reduce | flops 2097152 | bytes 12582912 | tf_op jit(solution)/shard_map/psum | solution.py:227
  409.3 0.0 reduce-scatter.4.cloned.1.call-done
  409.3 1.7 copy.6.right_side
  411.0 0.0 copy-start
  411.0 2.2 copy-done
  413.2 201.1 %shard_map.29 = f32[512,576]{1,0:T(8,128)S(1)} custom-call(bf16[512,4096]{1,0:T(8,128)(2,1)S(1)} %copy-done, f32[512,576]{1,0:T(8,128)S(1)} %copy.6.right_side), custom_call_target="tpu_custom_call" | custom-call | tf_op jit(solution)/shard_map/pallas_call | solution.py:243
  614.2 1.4 copy.4
  (1 shorter events, 0.0 us)
Async XLA Ops:
  6.5 402.8 %reduce-scatter.4.cloned.1.call-start = ((), (), s32[]{:S(2)}) async-start(), calls=%async_computation.1 | async-start | bytes 5898240
  6.5 7.9 %copy-start.1 = (bf16[1,512,2304]{2,1,0:T(8,128)(2,1)S(1)}, bf16[1,512,2304]{2,1,0:T(8,128)(2,1)}, u32[]{:S(2)}) copy-start(bf16[1,512,2304]{2,1,0:T(8,128)(2,1)} %param.3) | copy-start | bytes 7077892
  411.0 2.2 copy-start
Sparse Core Ops, SparseCore 0:
  237.4 71.7 reduce-scatter.3

commit v3 on v2

--- a/solution.py
+++ b/solution.py
@@ -132,15 +132,18 @@
     lax.fori_loop(0, lines, finish, 0)
 
 
-def weigh_kernel(lines, across, chunks, tile, gram, weights, total, full, recv_sem, line_sem, cross_sem):
+def weigh_kernel(lines, across, chunks, tile, gram, weights, out, full, total, recv_sem, line_sem, cross_sem):
     me = lax.axis_index("shard")
     full[me] = weights[...]
     total[...] = jnp.zeros_like(total)
     greet_all(lines * across)
     gather_multiply(lines, across, chunks, tile, gram, full, total, recv_sem, line_sem, cross_sem)
-
-
-def solve_kernel(lines, across, chunks, gram, right_side, merged, full, residual, direction, image,
+    width = out.shape[2]
+    for member in range(out.shape[0]):
+        out[member] = total[:, member * width:(member + 1) * width]
+
+
+def solve_kernel(lines, across, chunks, gram_sum, right_side, merged, gram, full, residual, direction, image,
                  product, sums, recv_sem, line_sem, cross_sem, sums_send, sums_recv):
     me = lax.axis_index("shard")
     count = lines * across
@@ -178,6 +181,7 @@
         return result
 
     greet_all(count)
+    gram[...] = gram_sum[...].astype(jnp.bfloat16)
     residual[...] = right_side[...]
     merged[...] = jnp.zeros_like(merged)
     norm_now = None
@@ -218,26 +222,34 @@
     return width
 
 
-def shards(lines, across, member_grams, member_weights):
+def shards(lines, across, members, member_grams, member_weights):
     height = member_grams.shape[1]
     features = member_weights.shape[2]
     count = lines * across
     regular = regularize(member_grams[0], lax.axis_index("shard") * height)
     gram_low = regular.astype(jnp.bfloat16)
-    gram_sum = lax.psum(regular, "member").astype(jnp.bfloat16)
+    gram_sum = lax.psum(regular, "member")
     vmem = pl.BlockSpec(memory_space=pltpu.VMEM)
     partial_rhs = pl.pallas_call(
         functools.partial(weigh_kernel, lines, across, 4, widest(features)),
-        out_shape=jax.ShapeDtypeStruct((height, features), jnp.float32),
+        out_shape=jax.ShapeDtypeStruct((members, height, features // members), jnp.float32),
         in_specs=[vmem, vmem],
         out_specs=vmem,
-        scratch_shapes=[pltpu.VMEM((count, height, features), jnp.bfloat16)]
+        scratch_shapes=[
+            pltpu.VMEM((count, height, features), jnp.bfloat16),
+            pltpu.VMEM((height, features), jnp.float32),
+        ]
         + gather_scratch(lines, across, 4),
         compiler_params=pltpu.CompilerParams(
             collective_id=0, has_side_effects=True, vmem_limit_bytes=48 << 20
         ),
+        cost_estimate=pl.CostEstimate(
+            flops=16 * count * height * height * features,
+            bytes_accessed=8 * count * height * features,
+            transcendentals=0,
+        ),
     )(gram_low, member_weights[0])
-    right_side = lax.psum_scatter(partial_rhs, "member", scatter_dimension=1, tiled=True)
+    right_side = lax.psum_scatter(partial_rhs, "member", scatter_dimension=0, tiled=False)
     width = right_side.shape[1]
     state = pltpu.VMEM((height, width), jnp.float32)
     return pl.pallas_call(
@@ -245,7 +257,10 @@
         out_shape=jax.ShapeDtypeStruct((height, width), jnp.float32),
         in_specs=[vmem, vmem],
         out_specs=vmem,
-        scratch_shapes=[pltpu.VMEM((count, height, width), jnp.bfloat16)]
+        scratch_shapes=[
+            pltpu.VMEM((height, count * height), jnp.bfloat16),
+            pltpu.VMEM((count, height, width), jnp.bfloat16),
+        ]
         + [state] * 4
         + [pltpu.VMEM((2 * ITERS, count, 8, width), jnp.float32)]
         + gather_scratch(lines, across, 2)
@@ -261,7 +276,7 @@
     places = {getattr(device, "coords", (0,))[0] for device in mesh.devices.flat}
     across = len(places) if count % len(places) == 0 else 1
     return jax.shard_map(
-        functools.partial(shards, count // across, across),
+        functools.partial(shards, count // across, across, mesh.shape["member"]),
         mesh=mesh,
         in_specs=(P("member", "shard", None), P("member", "shard", None)),
         out_specs=P("shard", "member"),

time: 623 us -> 497 us (0.80)
  blocking collectives: 172 us -> 0 us
  waiting for transfers between devices: 0.02 us -> 49.9 us
    psum x1 -> x0, blocking collectives: 172 us -> none  [shards(): gram_sum = lax.psum(regular, 'member').astype(jnp.bfloat16)]
    reduce_scatter x0 -> x1, waiting for transfers between devices: none -> 49.8 us  [shards(): lax.psum_scatter(partial_rhs, 'member', scatter_dimension=0, tiled=False)]
  transfers between devices with their start and end apart: 1 -> 2, of which waited for: 0 -> 1; matrix products, arithmetic and copies ran while one was open for 0% -> 0% of each run, Pallas kernels for 0% -> 44%
where the time goes in v3:
time: 497 us
  Pallas kernels  418 us (84%)
  waiting for transfers between devices  49.9 us (10%)
  between operations  13.4 us (3%)
  other arithmetic  7.72 us (2%)
  local copies, waits for them, and re-layouts  7.69 us (2%)
    pallas_call x1, Pallas kernels, shards(): pl.pallas_call(functools.partial(weigh_kernel, lines, across, 4, widest(f...  218 us
    pallas_call x1, Pallas kernels, shards(): pl.pallas_call(functools.partial(solve_kernel, lines, across, 2), out_sha...  201 us
    reduce_scatter x1, waiting for transfers between devices, shards(): lax.psum_scatter(partial_rhs, 'member', scatter_dimension=0, tiled=False)  49.8 us
  transfers between devices with their start and end apart: 2, of which 1 were waited for; matrix products, arithmetic and copies ran while one was open for 0% of the time, Pallas kernels for 44%

profile of v3, /device:TPU:0, one launch (start us, length us, event | category | flops | bytes accessed | tf_op | source)
XLA Modules:
  0.0 497.1 jit_solution(9978072007874382031)
XLA Ops:
  6.5 0.0 all-reduce.2.cloned.1.call-start
  6.5 7.7 %fusion = (bf16[512,4096]{1,0:T(8,128)(2,1)}, f32[512,4096]{1,0:T(8,128)}) fusion(f32[1,512,4096]{2,1,0:T(8,128)} %param.2, s32[512]{0:T(512)S(1)} %iota_add_fusion), kind=kLoop, calls=%fused_computation.3 | loop fusion | flops 8388608 | bytes 20973568 | tf_op jit(solution)/shard_map/convert_element_type | solution.py:230
  14.3 0.0 copy-start.2
  14.3 0.0 all-reduce.2.cloned.1.call-update
  14.3 0.0 reduce-scatter.2.cloned.1.call-start
  14.3 1.6 copy-done.2
  15.9 217.8 %shard_map.28 = f32[4,512,576]{2,1,0:T(8,128)} custom-call(bf16[512,4096]{1,0:T(8,128)(2,1)} %get-tuple-element.5.gram, bf16[512,2304]{1,0:T(8,128)(2,1)S(1)} %bitcast.6), custom_call_target="tpu_custom_call" | custom-call | flops 77309411328 | bytes 75497472 | tf_op jit(solution)/shard_map/pallas_call | solution.py:233
  233.7 0.0 reduce-scatter.2.cloned.1.call-update
  233.7 0.0 all-reduce.2.cloned.1.call-done.gram_sum
  233.8 49.8 %reduce-scatter.2.cloned.1.call-done = f32[1,512,576]{2,1,0:T(8,128)} async-done(((f32[4,512,576]{2,1,0:T(8,128)}), f32[1,512,576]{2,1,0:T(8,128)}) %reduce-scatter.2.cloned.1.call-update) | async-done | bytes 1179664 | tf_op jit(solution)/shard_map/reduce_scatter | solution.py:252
  283.6 0.0 copy-start
  283.6 3.4 copy-done
  286.9 0.0 copy-start.1
  286.9 1.3 copy-done.1
  288.3 200.6 %shard_map.29 = f32[512,576]{1,0:T(8,128)S(1)} custom-call(f32[512,4096]{1,0:T(8,128)S(1)} %copy-done, f32[512,576]{1,0:T(8,128)S(1)} %bitcast.5), custom_call_target="tpu_custom_call" | custom-call | tf_op jit(solution)/shard_map/pallas_call | solution.py:255
  488.9 1.4 copy.3
  (1 shorter events, 0.0 us)
Async XLA Ops:
  6.5 227.2 %all-reduce.2.cloned.1.call-start = ((), (), s32[]{:S(2)}) async-start(), calls=%async_computation.1 | async-start | bytes 16777216 | tf_op jit(solution)/shard_map/psum | solution.py:231
  14.3 1.7 copy-start.2
  14.3 269.3 %reduce-scatter.2.cloned.1.call-start = ((), (), s32[]{:S(2)}) async-start(), calls=%async_computation.2 | async-start | bytes 6553600 | tf_op jit(solution)/shard_map/reduce_scatter | solution.py:252
  283.6 3.4 copy-start
  286.9 1.3 copy-start.1
Sparse Core Ops, SparseCore 0:
  14.4 155.5 all-reduce.1
  233.9 49.6 reduce-scatter.1
